TPU v7x, 256 devices: a whole 4x4x8 slice. The times are simulated.
256 devices in a mesh: pa: 16 (over x, z_lo), pb: 16 (over z_hi, y, core).
Axes of the slice: x: 4, y: 4, z: 8 (z_hi: 2, z_lo: 4; z = z_hi * 4 + z_lo), core: 2. Of those that a mesh axis runs over, the one named last changes fastest.
Arguments:
- amplitudes: bfloat16 [384, 384, 2, 384], P('pa', 'pb'), may hold values from -6 to 6
- prev_slope: bfloat16 [384, 384, 2, 384], P('pa', 'pb'), may hold values from -6 to 6
- cholesky_vectors: bfloat16 [2304, 384, 384], P('pb', 'pa'), may hold values from -0.0625 to 0.0625
- energies: float32 [384], replicated, may hold values from -2 to 2
- occupations: float32 [384], replicated, may hold values from 0.02 to 0.98
Outputs:
- section_slope: bfloat16 [384, 384, 2, 384], P('pa', 'pb')
All inputs are finite; a program needn't handle non-finite values.
Results may differ from a plain program's by a relative error of at most 0.0063.
Values may be sent and summed in bfloat16 or wider, within the bound.
A program may use at most 128 MiB of HBM per device.

v0:
```python
import jax
import jax.numpy as jnp
from jax import lax
from jax.sharding import PartitionSpec as P


def mirror_section(tile_in):
    halfway = lax.all_to_all(
        lax.all_to_all(tile_in, "pa", split_axis=2, concat_axis=0, tiled=True),
        "pb",
        split_axis=0,
        concat_axis=1,
        tiled=True,
    )
    arrived = lax.all_to_all(halfway, "pa", split_axis=1, concat_axis=2, tiled=True)
    return jnp.swapaxes(arrived, 0, 1)


def blocked_terms(section_flat, fock_matrix, occupations):
    rows_a, rows_b, inner = section_flat.shape
    mirrored = mirror_section(section_flat)
    antisym = (section_flat.astype(jnp.float32) - mirrored.astype(jnp.float32)).astype(jnp.bfloat16)
    first_offset = lax.axis_index("pa") * rows_a
    second_offset = lax.axis_index("pb") * rows_b
    fock_first = lax.dynamic_slice_in_dim(fock_matrix, first_offset, rows_a, 0)
    flat_anti = antisym.reshape(rows_a, rows_b * inner)
    coeffs = fock_first
    left_term = jnp.dot(
        coeffs,
        lax.all_gather(flat_anti, "pa", axis=0, tiled=True),
        preferred_element_type=jnp.float32,
    )
    left_term = left_term.reshape(rows_a, rows_b, inner)
    fock_second = lax.dynamic_slice_in_dim(fock_matrix, second_offset, rows_b, 0)
    coeffs = fock_second
    right_term = jnp.einsum(
        "auk,bu->abk",
        lax.all_gather(antisym, "pb", axis=1, tiled=True),
        coeffs,
        preferred_element_type=jnp.float32,
    )
    occ_first = lax.dynamic_slice_in_dim(occupations, first_offset, rows_a)
    occ_second = lax.dynamic_slice_in_dim(occupations, second_offset, rows_b)
    factor = 1.0 - occ_first[:, None] - occ_second[None, :]
    return (-factor[:, :, None] * (left_term + right_term)).astype(jnp.bfloat16)


def shards(amplitudes, prev_slope, cholesky_vectors, energies, occupations):
    rows_a, rows_b, slab_depth, orbital_count = amplitudes.shape
    inner = slab_depth * orbital_count
    section_amps = (amplitudes.astype(jnp.float32) + 0.5 * prev_slope.astype(jnp.float32)).astype(
        jnp.bfloat16
    )
    section_flat = section_amps.reshape(rows_a, rows_b, inner)
    own_rows = cholesky_vectors.shape[1]
    local_occ = lax.dynamic_slice_in_dim(occupations, lax.axis_index("pa") * own_rows, own_rows)
    weighted = (
        cholesky_vectors.astype(jnp.float32) * (1.0 - 2.0 * local_occ)[None, :, None]
    ).astype(jnp.bfloat16)
    partial_sum = lax.dot_general(
        weighted, cholesky_vectors, (((0, 1), (0, 1)), ((), ())), preferred_element_type=jnp.float32
    )
    exchange = lax.psum(partial_sum, ("pa", "pb"))
    fock_matrix = (jnp.diag(energies) - exchange).astype(jnp.bfloat16)
    section_slope = blocked_terms(section_flat, fock_matrix, occupations)
    return section_slope.reshape(rows_a, rows_b, slab_depth, orbital_count)


def solution(mesh):
    in_specs = (P("pa", "pb", None, None), P("pa", "pb", None, None), P("pb", "pa", None), P(), P())
    out_specs = P("pa", "pb", None, None)
    return jax.shard_map(shards, mesh=mesh, in_specs=in_specs, out_specs=out_specs, check_vma=False)
```

profile of v0, /device:TPU:1, one launch (start us, length us, event | category | flops | bytes accessed | tf_op | source)
XLA Modules:
  0.0 693.0 jit_solution(6796999679026545356)
XLA Ops:
  7.4 2.6 add_convert_fusion
  9.9 0.6 reshape.48
  10.5 4.2 copy.13
  14.8 8.1 %reshape.56 = bf16[16,2,13824]{2,1,0:T(2,128)(2,1)S(1)} reshape(bf16[768,24,24]{2,1,0:T(8,128)(2,1)} %bitcast.46) | data formatting | bytes 1769472
  22.8 32.3 %all_to_all.45 = bf16[16,2,13824]{2,1,0:T(2,128)(2,1)S(1)} all-to-all(bf16[16,2,13824]{2,1,0:T(2,128)(2,1)S(1)} %reshape.56), channel_id=1, replica_groups=mesh['pa'=16,'pb'=16] {'pa'}, dimensions={0} | all-to-all | bytes 1769472 | tf_op jit(solution)/shard_map/all_to_all | solution.py:9
  55.1 7.7 %reshape.57 = bf16[768,24,24]{2,1,0:T(8,128)(2,1)} reshape(bf16[16,2,13824]{2,1,0:T(2,128)(2,1)S(1)} %all_to_all.45) | data formatting | bytes 1769472
  62.8 5.2 copy.14
  67.9 4.3 reshape.58
  72.2 35.1 %all_to_all.46 = bf16[16,2,13824]{2,1,0:T(2,128)(2,1)} all-to-all(bf16[16,2,13824]{2,1,0:T(2,128)(2,1)} %reshape.58), channel_id=1, replica_groups=mesh['pa'=16,'pb'=16] {'pb'}, dimensions={0} | all-to-all | bytes 1769472 | tf_op jit(solution)/shard_map/all_to_all | solution.py:8
  107.4 3.9 reshape.59
  111.3 0.6 copy.15
  111.9 1.5 copy.22
  113.5 0.0 copy-start.2
  113.5 4.3 reshape.60
  117.8 4.5 all-to-all-start.2
  122.3 0.0 all-reduce.2.cloned.1.call-start
  122.4 0.0 copy-done.2
  122.4 0.1 broadcast_subtract_fusion
  122.5 5.1 fusion.5
  127.5 0.0 all-reduce.2.cloned.1.call-update
  127.6 0.0 all-gather.3.cloned.1.call-start
  127.6 18.4 %all-to-all-done.2 = bf16[16,2,13824]{2,1,0:T(2,128)(2,1)} async-done(((bf16[16,2,13824]{2,1,0:T(2,128)(2,1)}), bf16[16,2,13824]{2,1,0:T(2,128)(2,1)}, u32[]{:S(2)}, u32[]{:S(2)}) %all-to-all-start.2) | async-done | bytes 884768 | tf_op jit(solution)/shard_map/all_to_all | solution.py:15
  146.0 3.9 reshape.61
  149.9 0.5 copy.17
  150.4 0.6 convert_bitcast_fusion
  151.0 3.0 copy.18
  154.0 5.2 reshape.52
  159.2 1.7 fusion.4
  160.9 0.0 copy-start
  160.9 0.0 copy-start.1
  160.9 1.2 copy.19
  162.1 0.0 all-gather.3.cloned.1.call-update
  162.1 0.3 all-gather.5.cloned.1.call-start
  162.4 0.0 copy-done
  162.4 0.3 all-gather.5.cloned.1.call-update
  162.7 0.1 subtract_negate_fusion
  162.8 506.8 %all-reduce.2.cloned.1.call-done = f32[384,384]{1,0:T(8,128)} async-done(((f32[384,384]{1,0:T(8,128)}), f32[384,384]{1,0:T(8,128)}) %all-reduce.2.cloned.1.call-update) | async-done | bytes 589840 | tf_op jit(solution)/shard_map/psum | solution.py:63
  669.5 0.0 copy-done.1
  669.5 1.2 subtract_convert_fusion
  670.7 0.0 all-gather.3.cloned.1.call-done
  670.8 6.1 fusion.8
  676.8 0.6 copy.20
  677.4 0.0 all-gather.5.cloned.1.call-done
  677.5 7.0 %fusion.3 = bf16[24,24,768]{2,1,0:T(8,128)(2,1)S(1)} fusion(f32[3,8,24,768]{3,2,1,0:T(8,128)S(1)} %copy.20, bf16[24,384,768]{2,1,0:T(8,128)(2,1)} %all-gather.5.cloned.1.call-done, f32[24,24]{1,0:T(8,128)S(1)} %subtract_negate_fusion, bf16[384,384]{1,0:T(8,128)(2,1)S(1)} %subtract_convert_fusion, s32[]{:T(128)S(6)} %select_n.15), kind=kOutput, calls=%fused_computation.6 | convolution fusion | flops 341065728 | bytes 16840708 | tf_op jit(solution)/shard_map/auk,bu->abk/dot_general | solution.py:36
  684.4 1.1 reshape.51
Async XLA Ops:
  113.5 8.9 %copy-start.2 = (f32[384]{0:T(512)S(1)}, f32[384]{0:T(512)}, u32[]{:S(2)}) copy-start(f32[384]{0:T(512)} %param.9) | copy-start | bytes 4612
  117.8 28.2 %all-to-all-start.2 = ((bf16[16,2,13824]{2,1,0:T(2,128)(2,1)}), bf16[16,2,13824]{2,1,0:T(2,128)(2,1)}, u32[]{:S(2)}, u32[]{:S(2)}) async-start(bf16[16,2,13824]{2,1,0:T(2,128)(2,1)} %reshape.60), calls=%async_computation.2 | async-start | bytes 1769472 | tf_op jit(solution)/shard_map/all_to_all | solution.py:15
  122.3 547.2 %all-reduce.2.cloned.1.call-start = ((), (), s32[]{:S(2)}) async-start(), calls=%async_computation.3 | async-start | bytes 1179648 | tf_op jit(solution)/shard_map/psum | solution.py:63
  127.6 543.2 %all-gather.3.cloned.1.call-start = ((), (), s32[]{:S(2)}) async-start(), calls=%async_computation.4 | async-start | bytes 15040512 | tf_op jit(solution)/shard_map/all_gather | solution.py:30
  160.9 1.5 copy-start
  160.9 508.7 %copy-start.1 = (f32[384]{0:T(512)S(1)}, f32[384]{0:T(512)}, u32[]{:S(2)}) copy-start(f32[384]{0:T(512)} %param.8) | copy-start | bytes 4612
  162.1 515.3 %all-gather.5.cloned.1.call-start = ((), (), s32[]{:S(2)}) async-start(), calls=%async_computation.5 | async-start | bytes 15040512 | tf_op jit(solution)/shard_map/all_gather | solution.py:38
Sparse Core Ops, SparseCore 0:
  128.7 540.8 all-reduce.1
Sparse Core Ops, SparseCore 1:
  162.2 296.5 all-gather.2
  461.7 155.2 all-gather.4
where the time goes:
time: 694 us; the launch traced here: 693 us
  waiting for transfers between devices  526 us (76%)
  blocking collectives  67.4 us (10%)
  local copies, waits for them, and re-layouts  55.9 us (8%)
  matrix products  18.1 us (3%)
  between operations  15 us (2%)
    psum x1, waiting for transfers between devices, shards(): exchange = lax.psum(partial_sum, ('pa', 'pb'))  507 us
    all_to_all x1, blocking collectives, mirror_section(): lax.all_to_all(lax.all_to_all(tile_in, 'pa', split_axis=2, concat_axis=0,...  35.1 us
    unnamed x14, local copies, waits for them, and re-layouts  34 us
    all_to_all x1, blocking collectives, mirror_section(): lax.all_to_all(tile_in, 'pa', split_axis=2, concat_axis=0, tiled=True)  32.3 us
    all_to_all x1, waiting for transfers between devices, mirror_section(): lax.all_to_all(halfway, 'pa', split_axis=1, concat_axis=2, tiled=True)  18.4 us
  transfers between devices with their start and end apart: 4, of which 2 were waited for; matrix products, arithmetic and copies ran while one was open for 4% of the time, Pallas kernels for 0%

commit v1 on v0

v1 whole, which is shorter than its diff:
```python
import functools

import jax
import jax.numpy as jnp
from jax import lax
from jax.experimental import pallas as pl
from jax.experimental.pallas import tpu as pltpu
from jax.sharding import PartitionSpec as P

N = 384
B = 24
K = 3


def place(j):
    pa = lax.axis_index("pa")
    pb = lax.axis_index("pb")
    x, y, z, c = pa // 4, (pb // 2) % 4, (pb // 8) * 4 + pa % 4, pb % 2
    dc, dz, dy, dx = j % 2, (j // 2) % 8, (j // 16) % 4, j // 64
    x, y, z, c = (x + dx) % 4, (y + dy) % 4, (z + dz) % 8, (c + dc) % 2
    return x * 4 + z % 4, (z // 4) * 8 + y * 2 + c


def exchange_kernel(spread, x_ref, o_ref, send, recv):
    me = lax.axis_index("pa") * 16 + lax.axis_index("pb")

    def step(j, _):
        qa, qb = place(j)
        source = x_ref.at[qa * 16 + qb] if spread else x_ref.at[0]
        pltpu.make_async_remote_copy(
            source, o_ref.at[me], send, recv, device_id=(qa, qb), device_id_type=pl.DeviceIdType.MESH
        ).start()
        return 0

    lax.fori_loop(1, 256, step, 0)
    o_ref[me] = x_ref[me] if spread else x_ref[0]
    part = o_ref.at[pl.ds(0, 255)]
    pltpu.make_async_copy(part, part, send).wait()
    pltpu.make_async_copy(part, part, recv).wait()


def exchange(x, spread=True):
    return pl.pallas_call(
        functools.partial(exchange_kernel, spread),
        out_shape=jax.ShapeDtypeStruct((256,) + x.shape[1:], x.dtype),
        in_specs=[pl.BlockSpec(memory_space=pltpu.VMEM)],
        out_specs=pl.BlockSpec(memory_space=pltpu.VMEM),
        scratch_shapes=[pltpu.SemaphoreType.DMA, pltpu.SemaphoreType.DMA],
        compiler_params=pltpu.CompilerParams(has_side_effects=True, vmem_limit_bytes=40 << 20),
    )(x)


def shards(amplitudes, prev_slope, cholesky_vectors, energies, occupations):
    pa, pb = lax.axis_index("pa"), lax.axis_index("pb")
    section = (amplitudes.astype(jnp.float32) + 0.5 * prev_slope.astype(jnp.float32)).astype(jnp.bfloat16)
    send = section.reshape(B * B, 256, K).transpose(1, 2, 0).reshape(256, K * B * B)
    send = jnp.pad(send, ((0, 0), (0, 2048 - K * B * B))).reshape(256, 16, 128)
    got = exchange(send).reshape(256, 2048)[:, : K * B * B]

    local_occ = lax.dynamic_slice_in_dim(occupations, pa * B, B)
    weighted = (cholesky_vectors.astype(jnp.float32) * (1.0 - 2.0 * local_occ)[None, :, None]).astype(jnp.bfloat16)
    partial = lax.dot_general(
        weighted, cholesky_vectors, (((0, 1), (0, 1)), ((), ())), preferred_element_type=jnp.float32
    )
    partial = jnp.pad(partial.reshape(256, 576), ((0, 0), (0, 448))).reshape(256, 8, 128)
    mine = exchange(partial).sum(axis=0, keepdims=True)
    total = exchange(mine, spread=False).reshape(256, 1024)[:, :576].reshape(N, N)
    fock = (jnp.diag(energies) - total).astype(jnp.bfloat16)

    s = got.reshape(16, 16, K, B, B).transpose(2, 0, 3, 1, 4).reshape(K, N, N)
    anti = (s.astype(jnp.float32) - jnp.swapaxes(s, 1, 2).astype(jnp.float32)).astype(jnp.bfloat16)
    left = jnp.einsum("pt,ktq->kpq", fock, anti, preferred_element_type=jnp.float32)
    right = jnp.einsum("kpu,qu->kpq", anti, fock, preferred_element_type=jnp.float32)
    factor = 1.0 - occupations[:, None] - occupations[None, :]
    out = (-factor[None] * (left + right)).astype(jnp.bfloat16)
    out = out.reshape(K, 16, B, 16, B).transpose(1, 3, 0, 2, 4).reshape(256, K * B * B)
    out = jnp.pad(out, ((0, 0), (0, 2048 - K * B * B))).reshape(256, 16, 128)
    back = exchange(out).reshape(256, 2048)[:, : K * B * B].reshape(768, B * B)
    return back.T.reshape(B, B, 2, N)


def solution(mesh):
    in_specs = (P("pa", "pb", None, None), P("pa", "pb", None, None), P("pb", "pa", None), P(), P())
    out_specs = P("pa", "pb", None, None)
    return jax.shard_map(shards, mesh=mesh, in_specs=in_specs, out_specs=out_specs, check_vma=False)
```

time: 694 us -> 236 us (0.34)
  waiting for transfers between devices: 526 us -> 0 us
  Pallas kernels: 0 us -> 159 us
  blocking collectives: 67.4 us -> 0 us
  between operations: 15 us -> 0.25 us
  matrix products: 18.1 us -> 5.73 us
  local copies, waits for them, and re-layouts: 55.9 us -> 65.3 us
    psum x1 -> x0, waiting for transfers between devices: 507 us -> none  [shards(): exchange = lax.psum(partial_sum, ('pa', 'pb'))]
    pallas_call x0 -> x4, Pallas kernels: none -> 159 us  [exchange(): pl.pallas_call(functools.partial(exchange_kernel, spread), out_shape=jax....]
    all_to_all x2 -> x0, blocking collectives: 67.4 us -> none  [the longest x1 35.1 us: mirror_section(): lax.all_to_all(lax.all_to_all(tile_in, 'pa', split_axis=2, concat_axis=0,...]
    unnamed x14 -> x11, local copies, waits for them, and re-layouts: 34 us -> 1.63 us
    reshape x3 -> x9, local copies, waits for them, and re-layouts: 5.91 us -> 31.5 us  [the longest x3 20.1 us: shards(): out.reshape(K, 16, B, 16, B).transpose(1, 3, 0, 2, 4)]
    convert_element_type x2 -> x5, local copies, waits for them, and re-layouts: 8.23 us -> 29.9 us  [the longest x4 23.9 us: shards(): s.astype(jnp.float32) - jnp.swapaxes(s, 1, 2).astype(jnp.float32)]
    all_to_all x1 -> x0, waiting for transfers between devices: 18.4 us -> none  [mirror_section(): lax.all_to_all(halfway, 'pa', split_axis=1, concat_axis=2, tiled=True)]
    dot_general x2, matrix products: 13.1 us -> 1.51 us  [the longest x1 0.77 us: shards(): jnp.einsum('pt,ktq->kpq', fock, anti, preferred_element_type=jnp.float32)]
  transfers between devices with their start and end apart: 4 -> 0, of which waited for: 2 -> 0; matrix products, arithmetic and copies ran while one was open for 4% -> 0% of each run, Pallas kernels for 0% -> 0%
where the time goes in v1:
time: 236 us; the launch traced here: 235 us
  Pallas kernels  159 us (67%)
  local copies, waits for them, and re-layouts  65.3 us (28%)
  matrix products  5.73 us (2%)
  other arithmetic  4.88 us (2%)
    pallas_call x4, Pallas kernels, exchange(): pl.pallas_call(functools.partial(exchange_kernel, spread), out_shape=jax....  159 us
    convert_element_type x4, local copies, waits for them, and re-layouts, shards(): s.astype(jnp.float32) - jnp.swapaxes(s, 1, 2).astype(jnp.float32)  23.9 us
    reshape x3, local copies, waits for them, and re-layouts, shards(): out.reshape(K, 16, B, 16, B).transpose(1, 3, 0, 2, 4)  20.1 us
    reshape x1, local copies, waits for them, and re-layouts, shards(): section.reshape(B * B, 256, K).transpose(1, 2, 0).reshape(256, K * B * B)  7.5 us
    convert_element_type x1, local copies, waits for them, and re-layouts, shards(): (amplitudes.astype(jnp.float32) + 0.5 * prev_slope.astype(jnp.float32)).a...  6.08 us

profile of v1, /device:TPU:1, one launch (start us, length us, event | category | flops | bytes accessed | tf_op | source)
XLA Modules:
  0.0 235.0 jit_solution(4924743860436909682)
XLA Ops:
  0.0 2.6 %add_convert_fusion = bf16[24,24,2,384]{3,2,1,0:T(2,128)(2,1)S(1)} fusion(bf16[24,24,2,384]{3,2,1,0:T(2,128)(2,1)} %param.6, bf16[24,24,2,384]{3,2,1,0:T(2,128)(2,1)} %param.5), kind=kLoop, calls=%fused_computation.8 | loop fusion | flops 2211840 | bytes 2654208 | tf_op jit(solution)/shard_map/convert_element_type | solution.py:55
  2.6 6.1 %copy.25 = bf16[24,24,2,384]{1,0,3,2:T(8,128)(2,1)} copy(bf16[24,24,2,384]{3,2,1,0:T(2,128)(2,1)S(1)} %add_convert_fusion) | data formatting | bytes 1769472 | tf_op jit(solution)/shard_map/convert_element_type | solution.py:55
  8.7 7.5 %reshape.84 = bf16[576,256,3]{0,2,1:T(4,128)(2,1)S(1)} reshape(bf16[24,24,2,384]{1,0,3,2:T(8,128)(2,1)} %copy.25) | data formatting | bytes 1769472 | tf_op jit(solution)/shard_map/reshape | solution.py:56
  16.2 1.4 copy.26
  17.6 0.1 pad.11
  17.7 1.1 copy.36.x_ref
  18.8 46.1 %shard_map.55 = bf16[256,16,128]{2,1,0:T(8,128)(2,1)S(1)} custom-call(bf16[256,16,128]{2,1,0:T(8,128)(2,1)S(1)} %copy.36.x_ref), custom_call_target="tpu_custom_call" | custom-call | tf_op jit(solution)/shard_map/pallas_call | solution.py:43
  64.9 0.3 copy.47
  65.2 0.1 slice_convert_fusion
  65.4 5.5 %reshape.100 = f32[16,16,3,24,24]{4,3,2,1,0:T(8,128)} reshape(f32[256,1728]{1,0:T(8,128)S(1)} %slice_convert_fusion) | data formatting | bytes 3538944 | tf_op jit(solution)/shard_map/convert_element_type | solution.py:71
  70.8 9.3 %copy.28 = f32[3,16,24,16,24]{4,3,2,1,0:T(8,128)} copy(f32[3,16,24,16,24]{4,2,0,3,1:T(8,128)} %bitcast.60) | data formatting | bytes 3538944 | tf_op jit(solution)/shard_map/convert_element_type | solution.py:71
  80.1 7.3 %reshape.98 = f32[3,384,384]{2,1,0:T(8,128)S(1)} reshape(f32[3,16,24,16,24]{4,3,2,1,0:T(8,128)} %copy.28) | data formatting | bytes 3538944 | tf_op jit(solution)/shard_map/convert_element_type | solution.py:71
  87.4 1.8 copy.29
  89.2 0.0 copy-start
  89.2 1.7 fusion.4
  90.9 0.0 copy-done
  90.9 0.1 multiply_subtract_fusion
  91.0 4.2 %fusion.5 = f32[384,384]{1,0:T(8,128)S(1)} fusion(bf16[144,24,384]{2,1,0:T(8,128)(2,1)} %param.7, f32[24]{0:T(128)S(1)} %multiply_subtract_fusion), kind=kOutput, calls=%fused_computation.9 | convolution fusion | flops 1023197184 | bytes 3244128 | tf_op jit(solution)/shard_map/dot_general | solution.py:62
  95.2 0.3 reshape.88
  95.6 0.1 pad_bitcast_fusion.1
  95.7 0.2 copy.38
  95.9 37.7 %shard_map.56 = f32[256,8,128]{2,1,0:T(8,128)S(1)} custom-call(f32[256,8,128]{2,1,0:T(8,128)S(1)} %bitcast.55), custom_call_target="tpu_custom_call" | custom-call | tf_op jit(solution)/shard_map/pallas_call | solution.py:43
  133.7 0.3 reduce_sum.9
  133.9 37.4 %shard_map.57 = f32[256,8,128]{2,1,0:T(8,128)S(1)} custom-call(f32[1,8,128]{2,1,0:T(8,128)S(1)} %bitcast.59), custom_call_target="tpu_custom_call" | custom-call | tf_op jit(solution)/shard_map/pallas_call | solution.py:43
  171.3 0.2 copy.46
  171.5 0.0 copy-start.1
  171.5 0.1 slice.13
  171.6 0.4 reshape.91
  172.0 0.2 copy-done.1
  172.2 0.8 fusion.8
  173.0 0.1 subtract_negate_fusion
  173.1 0.7 fusion.3
  173.9 7.1 %reshape.92 = bf16[3,16,24,16,24]{2,1,4,3,0:T(8,128)(2,1)} reshape(bf16[3,384,384]{1,2,0:T(8,128)(2,1)S(1)} %fusion.3) | data formatting | bytes 1769472 | tf_op jit(solution)/shard_map/reshape | solution.py:76
  180.9 7.2 %copy.32 = bf16[3,16,24,16,24]{4,2,0,3,1:T(8,128)(2,1)} copy(bf16[3,16,24,16,24]{2,1,4,3,0:T(8,128)(2,1)} %reshape.92) | data formatting | bytes 1769472 | tf_op jit(solution)/shard_map/reshape | solution.py:76
  188.2 5.8 %reshape.93 = bf16[256,1728]{1,0:T(8,128)(2,1)S(1)} reshape(bf16[16,16,3,24,24]{4,3,2,1,0:T(8,128)(2,1)} %bitcast.61) | data formatting | bytes 1769472 | tf_op jit(solution)/shard_map/reshape | solution.py:76
  194.0 0.1 pad_bitcast_fusion
  194.1 0.2 copy.40
  194.4 37.5 %shard_map.58 = bf16[256,16,128]{2,1,0:T(8,128)(2,1)S(1)} custom-call(bf16[256,16,128]{2,1,0:T(8,128)(2,1)S(1)} %bitcast.57), custom_call_target="tpu_custom_call" | custom-call | tf_op jit(solution)/shard_map/pallas_call | solution.py:43
  231.9 0.3 copy.45
  232.2 0.1 slice.14
  232.3 1.0 reshape.96
  233.3 0.6 copy.33
  233.9 1.1 reshape.97
  (1 shorter events, 0.0 us)
Async XLA Ops:
  89.2 1.7 copy-start
  171.5 0.7 copy-start.1

commit v2 on v1

v2 whole, which is shorter than its diff:
```python
import functools

import jax
import jax.numpy as jnp
from jax import lax
from jax.experimental import pallas as pl
from jax.experimental.pallas import tpu as pltpu
from jax.sharding import PartitionSpec as P

N = 384
B = 24
K = 3
BB = B * B
D = 256
F32 = jnp.float32
BF16 = jnp.bfloat16
MESH = pl.DeviceIdType.MESH


def place():
    pa = lax.axis_index("pa")
    pb = lax.axis_index("pb")
    return pa // 4, (pb // 2) % 4, (pb // 8) * 4 + pa % 4, pb % 2


def device(x, y, z, c):
    return x * 4 + z % 4, (z // 4) * 8 + y * 2 + c


def partner(j):
    x, y, z, c = place()
    dc, dz, dy, dx = j % 2, (j // 2) % 8, (j // 16) % 4, j // 64
    return device((x + dx) % 4, (y + dy) % 4, (z + dz) % 8, (c + dc) % 2)


def iota(shape, axis):
    return lax.broadcasted_iota(jnp.int32, shape, axis)


def one_hot(mask):
    return jnp.where(mask, 1.0, 0.0).astype(BF16)


def dot(a, b):
    return jnp.dot(a, b, preferred_element_type=F32)


def dot_t(a, b):
    return lax.dot_general(a, b, (((1,), (1,)), ((), ())), preferred_element_type=F32)


def pack(z, mix, buf):
    for u in range(7):
        pair = jnp.concatenate(
            [z[256 * u : 256 * u + 128, :], z[256 * u + 128 : 256 * u + 256, :]], axis=1
        ).astype(BF16)
        rows = dot_t(mix[...], pair).astype(BF16)
        buf[:, u] = rows.reshape(D, 2, 128)


def unpack(buf, mix_t, eye, z):
    for u in range(7):
        rows = buf[:, u].reshape(2 * D, 128)
        parted = dot(mix_t[...], rows).astype(BF16)
        turned = dot_t(eye, parted)
        z[256 * u : 256 * u + 128, :] = turned[:, :D].astype(z.dtype)
        z[256 * u + 128 : 256 * u + 256, :] = turned[:, D:].astype(z.dtype)


def turn_blocks(xs):
    xs = list(xs)
    block = iota(xs[0].shape, 1) // 16
    for w in (1, 2, 4):
        high = (block & w) != 0
        for i in range(8):
            if i & w == 0:
                a, b = xs[i], xs[i + w]
                xs[i] = jnp.where(high, pltpu.roll(b, 16 * w, 1), a)
                xs[i + w] = jnp.where(high, b, pltpu.roll(a, 128 - 16 * w, 1))
    return xs


def kernel(amp, prev, chol, hole, energies, factor, out,
           z16, z32, mix, mix_t, send1, recv1, send2, recv2, mats, holes,
           partial, half, sums, from_core, from_y, from_z, from_x, rows48, fock, sems, rsems):
    x, y, z, c = place()
    me_a, me_b = device(x, y, z, c)
    me = me_b * 16 + me_a

    barrier = pltpu.get_barrier_semaphore()

    def greet(j, _):
        pl.semaphore_signal(barrier, inc=1, device_id=partner(j), device_id_type=MESH)
        return 0

    lax.fori_loop(1, D, greet, 0)

    def start(source, target, stage, where):
        pltpu.make_async_remote_copy(
            source, target, sems.at[stage], rsems.at[stage], device_id=where, device_id_type=MESH
        ).start()

    def wait(sem, like):
        pltpu.make_async_copy(like, like, sem).wait()

    def ship(lo, hi, source, target, stage):
        def step(j, _):
            qa, qb = partner(j)
            start(source.at[qb * 16 + qa], target.at[me], stage, (qa, qb))
            return 0

        lax.fori_loop(lo, hi, step, 0)

    r, q = iota((512, 512), 0), iota((512, 512), 1)
    mix[...] = one_hot(r // 2 + (r % 2) * D == q)
    mix_t[...] = one_hot(q // 2 + (q % 2) * D == r)
    eye = one_hot(iota((128, 128), 0) == iota((128, 128), 1))

    for i in range(0, BB, 64):
        s = amp[i : i + 64].astype(F32) + 0.5 * prev[i : i + 64].astype(F32)
        s = s.reshape(64, 2 * N).astype(BF16)
        for j in range(K):
            z16[j * BB + i : j * BB + i + 64, :] = s[:, j * D : (j + 1) * D]
    z16[K * BB :, :] = jnp.zeros((64, D), BF16)
    pack(z16, mix, send1)
    send1_own = send1[pl.ds(me, 1)]
    recv1[pl.ds(me, 1)] = send1_own

    pl.semaphore_wait(barrier, D - 1)
    ship(1, 64, send1, recv1, 0)

    for i in range(16):
        holes[i * B : (i + 1) * B, :] = hole[...]
    partial[...] = jnp.zeros((N, N), F32)

    def rank_rows(i, _):
        rows = chol[pl.ds(pl.multiple_of(i * N, N), N), :]
        weighted = (rows.astype(F32) * holes[...]).astype(BF16)
        partial[...] += lax.dot_general(
            weighted, rows, (((0,), (0,)), ((), ())), preferred_element_type=F32
        )
        return 0

    lax.fori_loop(0, 9, rank_rows, 0)

    start(partial.at[pl.ds(192 * (1 - c), 192)], from_core, 1, device(x, y, z, 1 - c))
    ship(64, 128, send1, recv1, 0)
    wait(rsems.at[1], from_core)
    half[...] = partial[pl.ds(192 * c, 192), :] + from_core[...]
    for d in (1, 2, 3):
        y2 = (y + d) % 4
        start(half.at[pl.ds(48 * y2, 48)], from_y.at[y], 2, device(x, y2, z, c))
    from_y[pl.ds(y, 1)] = half[pl.ds(48 * y, 48), :][None]
    ship(128, 176, send1, recv1, 0)
    wait(rsems.at[2], from_y.at[pl.ds(0, 3)])
    sums[...] = from_y[0] + from_y[1] + from_y[2] + from_y[3]
    for d in range(1, 8):
        z2 = (z + d) % 8

        @pl.when(z2 < 6)
        def _():
            start(sums.at[pl.ds(8 * z2, 8)], from_z.at[z], 3, device(x, y, z2, c))

    ship(176, 216, send1, recv1, 0)

    @pl.when(z < 6)
    def _():
        from_z[pl.ds(z, 1)] = sums[pl.ds(8 * z, 8), :][None]
        wait(rsems.at[3], from_z.at[pl.ds(0, 7)])
        total = from_z[0]
        for d in range(1, 8):
            total = total + from_z[d]
        from_x[pl.ds(x, 1)] = total[None]
        for d in (1, 2, 3):
            x2 = (x + d) % 4
            start(from_x.at[x], from_x.at[x], 4, device(x2, y, z, c))

    ship(216, D, send1, recv1, 0)

    @pl.when(z < 6)
    def _():
        wait(rsems.at[4], from_x.at[pl.ds(0, 3)])
        rows48[pl.ds(8 * z, 8), :] = from_x[0] + from_x[1] + from_x[2] + from_x[3]
        for d in range(1, 8):
            mine = rows48.at[pl.ds(8 * z, 8)]
            start(mine, mine, 5, device(x, y, (z + d) % 8, c))
        wait(rsems.at[5], rows48.at[pl.ds(0, 40)])

    @pl.when(z >= 6)
    def _():
        wait(rsems.at[5], rows48)

    first = 192 * c + 48 * y
    diagonal = jnp.where(iota((48, N), 0) + first == iota((48, N), 1), energies[...], 0.0)
    fock[pl.ds(pl.multiple_of(first, 48), 48), :] = (diagonal - rows48[...]).astype(BF16)
    mine = fock.at[pl.ds(pl.multiple_of(first, 48), 48)]
    for d in (1, 2, 3):
        start(mine, mine, 6, device(x, (y + d) % 4, z, c))
    wait(rsems.at[6], fock.at[pl.ds(0, 144)])
    mine = fock.at[pl.ds(pl.multiple_of(192 * c, 192), 192)]
    start(mine, mine, 7, device(x, y, z, 1 - c))
    wait(rsems.at[7], mine)

    wait(rsems.at[0], recv1.at[pl.ds(0, D - 1)])
    unpack(recv1, mix_t, eye, z32)
    for j in range(K):
        for pg in range(3):
            for bg in range(2):
                rows = [j * BB + (pg * 8 + i) * B for i in range(8)]
                got = turn_blocks([z32[h : h + B, bg * 128 : bg * 128 + 128] for h in rows])
                for i in range(8):
                    h = (bg * 8 + i) * B
                    mats[j, h : h + B, pg * 128 : pg * 128 + 128] = got[i]

    lane, p = iota((N, N), 0), iota((N, N), 1)
    order_t = one_hot((lane % 16) * B + lane // 16 == p)
    order = one_hot((p % 16) * B + p // 16 == lane)
    for j in range(K):
        held = mats[j].astype(BF16)
        anti = (dot_t(order, held) - dot(held, order_t)).astype(BF16)
        both = dot(fock[...], anti) + dot_t(anti, fock[...])
        slope = (factor[...] * both).astype(BF16)
        mats[j] = dot(slope, order)
        for pg in range(3):
            for bg in range(2):
                rows = [(bg * 8 + i) * B for i in range(8)]
                got = turn_blocks([mats[j, h : h + B, pg * 128 : pg * 128 + 128] for h in rows])
                for i in range(8):
                    h = j * BB + (pg * 8 + i) * B
                    z32[h : h + B, bg * 128 : bg * 128 + 128] = got[i]
    pack(z32, mix, send2)
    recv2[pl.ds(me, 1)] = send2[pl.ds(me, 1)]
    ship(1, D, send2, recv2, 8)
    wait(rsems.at[8], recv2.at[pl.ds(0, D - 1)])
    unpack(recv2, mix_t, eye, z16)
    for i in range(0, BB, 64):
        s = jnp.concatenate([z16[j * BB + i : j * BB + i + 64, :] for j in range(K)], axis=1)
        out[i : i + 64] = s.reshape(64, 2, N)

    wait(sems.at[0], send1.at[pl.ds(0, D - 1)])
    wait(sems.at[1], from_core)
    wait(sems.at[2], from_y.at[pl.ds(0, 3)])

    @pl.when(z < 6)
    def _():
        wait(sems.at[3], from_z.at[pl.ds(0, 5)])
        wait(sems.at[4], from_x.at[pl.ds(0, 3)])
        wait(sems.at[5], from_z.at[pl.ds(0, 7)])

    @pl.when(z >= 6)
    def _():
        wait(sems.at[3], from_z.at[pl.ds(0, 6)])

    wait(sems.at[6], fock.at[pl.ds(0, 144)])
    wait(sems.at[7], fock.at[pl.ds(0, 192)])
    wait(sems.at[8], send2.at[pl.ds(0, D - 1)])


def shards(amplitudes, prev_slope, cholesky_vectors, energies, occupations):
    pa = lax.axis_index("pa")
    local_occ = lax.dynamic_slice_in_dim(occupations, pa * B, B)
    hole = jnp.broadcast_to((1.0 - 2.0 * local_occ)[:, None], (B, N))
    factor = 1.0 - occupations[:, None] - occupations[None, :]
    vmem = pl.BlockSpec(memory_space=pltpu.VMEM)
    slope = pl.pallas_call(
        kernel,
        out_shape=jax.ShapeDtypeStruct((BB, 2, N), BF16),
        in_specs=[vmem] * 6,
        out_specs=vmem,
        scratch_shapes=[
            pltpu.VMEM((1792, D), BF16),
            pltpu.VMEM((1792, D), F32),
            pltpu.VMEM((512, 512), BF16),
            pltpu.VMEM((512, 512), BF16),
            pltpu.VMEM((D, 7, 2, 128), BF16),
            pltpu.VMEM((D, 7, 2, 128), BF16),
            pltpu.VMEM((D, 7, 2, 128), BF16),
            pltpu.VMEM((D, 7, 2, 128), BF16),
            pltpu.VMEM((K, N, N), F32),
            pltpu.VMEM((N, N), F32),
            pltpu.VMEM((N, N), F32),
            pltpu.VMEM((192, N), F32),
            pltpu.VMEM((48, N), F32),
            pltpu.VMEM((192, N), F32),
            pltpu.VMEM((4, 48, N), F32),
            pltpu.VMEM((8, 8, N), F32),
            pltpu.VMEM((4, 8, N), F32),
            pltpu.VMEM((48, N), F32),
            pltpu.VMEM((N, N), BF16),
            pltpu.SemaphoreType.DMA((9,)),
            pltpu.SemaphoreType.DMA((9,)),
        ],
        compiler_params=pltpu.CompilerParams(
            collective_id=0, has_side_effects=True, vmem_limit_bytes=56 << 20
        ),
    )(
        amplitudes.reshape(BB, 2, N),
        prev_slope.reshape(BB, 2, N),
        cholesky_vectors.reshape(-1, N),
        hole,
        energies.reshape(1, N),
        factor,
    )
    return slope.reshape(B, B, 2, N)


def solution(mesh):
    in_specs = (P("pa", "pb", None, None), P("pa", "pb", None, None), P("pb", "pa", None), P(), P())
    out_specs = P("pa", "pb", None, None)
    return jax.shard_map(shards, mesh=mesh, in_specs=in_specs, out_specs=out_specs, check_vma=False)
```

time: 236 us -> 105 us (0.44)
  Pallas kernels: 159 us -> 97.4 us
  local copies, waits for them, and re-layouts: 65.3 us -> 4.63 us
  matrix products: 5.73 us -> 0 us
    pallas_call x4 -> x1, Pallas kernels: 159 us -> 97.4 us  [shards(): pl.pallas_call(kernel, out_shape=jax.ShapeDtypeStruct((BB, 2, N), BF16),...]
    reshape x9 -> x1, local copies, waits for them, and re-layouts: 31.5 us -> 1.26 us  [shards(): energies.reshape(1, N)]
    convert_element_type x5 -> x0, local copies, waits for them, and re-layouts: 29.9 us -> none  [the longest x4 23.9 us: shards(): s.astype(jnp.float32) - jnp.swapaxes(s, 1, 2).astype(jnp.float32)]
    dot_general x3 -> x0, matrix products: 5.73 us -> none  [the longest x1 4.22 us: shards(): lax.dot_general(weighted, cholesky_vectors, (((0, 1), (0, 1)), ((), ())),...]
    convert_element_type x3 -> x0, other arithmetic: 4.41 us -> none  [the longest x1 2.57 us: shards(): (amplitudes.astype(jnp.float32) + 0.5 * prev_slope.astype(jnp.float32)).a...]
where the time goes in v2:
time: 105 us
  Pallas kernels  97.4 us (93%)
  local copies, waits for them, and re-layouts  4.63 us (4%)
  other arithmetic  3.05 us (3%)
    pallas_call x1, Pallas kernels, shards(): pl.pallas_call(kernel, out_shape=jax.ShapeDtypeStruct((BB, 2, N), BF16),...  97.4 us
    unnamed x1, local copies, waits for them, and re-layouts  2.69 us
    sub x2, other arithmetic, shards(): factor = 1.0 - occupations[:, None] - occupations[None, :]  2.3 us

profile of v2, /device:TPU:1, one launch (start us, length us, event | category | flops | bytes accessed | tf_op | source)
XLA Modules:
  0.0 105.1 jit_solution(12480563351398603963)
XLA Ops:
  0.0 0.8 multiply_subtract_fusion
  0.8 1.3 %reshape.22.energies = f32[1,384]{1,0:T(1,128)} reshape(f32[384]{0:T(512)} %param.8) | data formatting | bytes 3072 | tf_op jit(solution)/shard_map/reshape | solution.py:301
  2.0 0.7 broadcast_subtract_fusion.1
  2.7 0.7 broadcast_in_dim.2.hole
  3.4 1.6 %broadcast_subtract_fusion.factor = f32[384,384]{1,0:T(8,128)} fusion(f32[384]{0:T(512)} %param.9, f32[384]{0:T(512)S(1)} %broadcast_subtract_fusion.1), kind=kLoop, calls=%fused_computation | loop fusion | flops 147456 | bytes 592896 | tf_op jit(solution)/shard_map/sub | solution.py:263
  5.0 97.4 %shard_map.55 = bf16[576,2,384]{2,1,0:T(2,128)(2,1)} custom-call(bf16[576,2,384]{2,1,0:T(2,128)(2,1)} %bitcast.6, bf16[576,2,384]{2,1,0:T(2,128)(2,1)} %bitcast.7, bf16[3456,384]{1,0:T(8,128)(2,1)} %bitcast.5, f32[24,384]{1,0:T(8,128)} %broadcast_in_dim.2.hole, f32[1,384]{1,0:T(1,128)} %reshape.22.energies, f32[384,384]{1,0:T(8,128)} %broadcast_subtract_fusion.factor), custom_call_target="tpu_custom_call" | custom-call | tf_op jit(solution)/shard_map/pallas_call | solution.py:265
  102.4 2.7 %copy.7 = bf16[24,24,2,384]{3,2,1,0:T(2,128)(2,1)} copy(bf16[24,24,2,384]{3,2,1,0:T(2,128)(2,1)} %bitcast.4) | data formatting | bytes 1769472

commit v3 on v2

v3 whole, which is shorter than its diff:
```python
import jax
import jax.numpy as jnp
from jax import lax
from jax.experimental import pallas as pl
from jax.experimental.pallas import tpu as pltpu
from jax.sharding import PartitionSpec as P

N = 384
B = 24
K = 3
BB = B * B
D = 256
UNITS = 7
F32 = jnp.float32
BF16 = jnp.bfloat16
MESH = pl.DeviceIdType.MESH
IN_PARTS = ((0, 3), (3, 2), (5, 2))
OUT_PARTS = ((0, 2), (2, 2), (4, 3))


def place():
    pa = lax.axis_index("pa")
    pb = lax.axis_index("pb")
    return pa >> 2, (pb >> 1) & 3, ((pb >> 3) << 2) | (pa & 3), pb & 1


def device(x, y, z, c):
    return (x << 2) | (z & 3), ((z >> 2) << 3) | (y << 1) | c


def partner(j):
    x, y, z, c = place()
    return device((x + (j >> 6)) & 3, (y + ((j >> 4) & 3)) & 3, (z + ((j >> 1) & 7)) & 7, (c + j) & 1)


def iota(shape, axis):
    return lax.broadcasted_iota(jnp.int32, shape, axis)


def one_hot(mask):
    return jnp.where(mask, 1.0, 0.0).astype(BF16)


def dot(a, b):
    return jnp.dot(a, b, preferred_element_type=F32)


def dot_t(a, b):
    return lax.dot_general(a, b, (((1,), (1,)), ((), ())), preferred_element_type=F32)


def row_home(rho):
    return ((rho >> 1) & 15) * B + (rho >> 5) * 2 + (rho & 1)


def lane_home(kappa):
    return ((kappa >> 3) & 15) * B + (kappa >> 7) * 8 + (kappa & 7)


def turn_blocks(xs, lane):
    xs = list(xs)
    for w in (1, 2, 4, 8):
        high = (lane & (8 * w)) != 0
        for i in range(16):
            if i & w == 0:
                a, b = xs[i], xs[i + w]
                xs[i] = jnp.where(high, pltpu.roll(b, 8 * w, 1), a)
                xs[i + w] = jnp.where(high, b, pltpu.roll(a, 128 - 8 * w, 1))
    return xs


def kernel(amp_hbm, prev_hbm, chol_hbm, energies, occ, out,
           amp, prev, chol, zs, mix, mix_t, send1, recv1, send2, recv2, mats, outs, holes,
           partial, half, sums, from_core, from_y, from_z, from_x, rows48, fock, fock_p, factor, turn, turn_t,
           greet, loads, sems, rsems):
    x, y, z, c = place()
    me_a, me_b = device(x, y, z, c)
    me = (me_b << 4) | me_a

    load_amp = pltpu.make_async_copy(amp_hbm, amp, loads.at[0])
    load_prev = pltpu.make_async_copy(prev_hbm, prev, loads.at[1])
    load_chol = pltpu.make_async_copy(chol_hbm, chol, loads.at[2])
    load_amp.start()
    load_prev.start()
    load_chol.start()

    barrier = pltpu.get_barrier_semaphore()
    column = [device(x, y, (z + d) & 7, c ^ e) for d in range(8) for e in range(2) if d or e]
    plane = [device((x + d) & 3, (y + e) & 3, z, c) for d in range(4) for e in range(4) if d or e]
    for where in column + plane:
        pl.semaphore_signal(barrier, inc=1, device_id=where, device_id_type=MESH)

    def start(source, target, stage, where):
        pltpu.make_async_remote_copy(
            source, target, sems.at[stage], rsems.at[stage], device_id=where, device_id_type=MESH
        ).start()

    def wait(sem, like):
        pltpu.make_async_copy(like, like, sem).wait()

    def ship(lo, hi, part, source, target, stage):
        units = pl.ds(part[0], part[1])

        def step(j, _):
            qa, qb = partner(j)
            start(source.at[units, (qb << 4) | qa], target.at[units, me], stage, (qa, qb))
            return 0

        lax.fori_loop(lo, hi, step, 0)

    def all_but_one(buf, part):
        return buf.at[pl.ds(part[0], part[1]), pl.ds(0, D - 1)]

    r, q = iota((512, 512), 0), iota((512, 512), 1)
    mix[...] = one_hot((r >> 1) + (r & 1) * D == q)
    mix_t[...] = one_hot((q >> 1) + (q & 1) * D == r)
    eye = one_hot(iota((128, 128), 0) == iota((128, 128), 1))

    load_amp.wait()
    load_prev.wait()
    for h in range(0, BB, 3 * B):
        s = amp[h : h + 3 * B].astype(F32) + 0.5 * prev[h : h + 3 * B].astype(F32)
        s = s.reshape(3 * B, 2 * N)
        for t in range(0, 3 * B, 8):
            p, g = (h + t) // B, ((h + t) % B) // 8
            for j in range(K):
                at = ((j * 3 + g) * 12 + p // 2) * 8
                zs[p % 2, at : at + 8, :] = s[t : t + 8, j * D : (j + 1) * D]
    for i in range(2):
        zs[i, 3 * BB // 2 :, :] = jnp.zeros((32, D), F32)
    folded = send1.reshape(UNITS, 2 * D, 128)
    for u in range(UNITS):
        pair = jnp.concatenate([zs[i, 128 * u : 128 * u + 128, :] for i in range(2)], axis=1).astype(BF16)
        folded[u] = dot_t(mix[...], pair).astype(BF16)
    recv1[:, pl.ds(me, 1)] = send1[:, pl.ds(me, 1)]

    pl.semaphore_wait(barrier, len(column + plane))
    for where in plane:
        pl.semaphore_signal(greet, inc=1, device_id=where, device_id_type=MESH)
    pl.semaphore_wait(greet, len(plane))
    ship(1, D, IN_PARTS[0], send1, recv1, 0)

    spread = jnp.broadcast_to(occ[...], (128, N))
    upright = jnp.transpose(spread)
    partial[:, 0:128] = upright
    hole = 1.0 - 2.0 * partial[pl.ds(pl.multiple_of(me_a * B, 8), B), 0:128]
    for i in range(16):
        for t in range(3):
            holes[i * B : (i + 1) * B, t * 128 : t * 128 + 128] = hole
    load_chol.wait()
    partial[...] = jnp.zeros((N, N), F32)

    def rank_rows(i, _):
        rows = chol[pl.ds(pl.multiple_of(i * N, N), N), :]
        weighted = (rows.astype(F32) * holes[...]).astype(BF16)
        partial[...] += lax.dot_general(
            weighted, rows, (((0,), (0,)), ((), ())), preferred_element_type=F32
        )
        return 0

    lax.fori_loop(0, 9, rank_rows, 0)

    start(partial.at[pl.ds(192 * (1 - c), 192)], from_core, 6, device(x, y, z, 1 - c))
    ship(1, 64, IN_PARTS[1], send1, recv1, 1)
    wait(rsems.at[6], from_core)
    half[...] = partial[pl.ds(192 * c, 192), :] + from_core[...]
    for d in (1, 2, 3):
        y2 = (y + d) & 3
        start(half.at[pl.ds(48 * y2, 48)], from_y.at[y], 7, device(x, y2, z, c))
    from_y[pl.ds(y, 1)] = half[pl.ds(48 * y, 48), :][None]
    ship(64, 192, IN_PARTS[1], send1, recv1, 1)
    wait(rsems.at[7], from_y.at[pl.ds(0, 3)])
    sums[...] = from_y[0] + from_y[1] + from_y[2] + from_y[3]
    for d in range(1, 8):
        z2 = (z + d) & 7

        @pl.when(z2 < 6)
        def _():
            start(sums.at[pl.ds(8 * z2, 8)], from_z.at[z], 8, device(x, y, z2, c))

    ship(192, D, IN_PARTS[1], send1, recv1, 1)

    @pl.when(z < 6)
    def _():
        from_z[pl.ds(z, 1)] = sums[pl.ds(8 * z, 8), :][None]
        wait(rsems.at[8], from_z.at[pl.ds(0, 7)])
        total = from_z[0]
        for d in range(1, 8):
            total = total + from_z[d]
        from_x[pl.ds(x, 1)] = total[None]
        for d in (1, 2, 3):
            start(from_x.at[x], from_x.at[x], 9, device((x + d) & 3, y, z, c))

    ship(1, 64, IN_PARTS[2], send1, recv1, 2)

    @pl.when(z < 6)
    def _():
        wait(rsems.at[9], from_x.at[pl.ds(0, 3)])
        rows48[pl.ds(8 * z, 8), :] = from_x[0] + from_x[1] + from_x[2] + from_x[3]
        for d in range(1, 8):
            mine = rows48.at[pl.ds(8 * z, 8)]
            start(mine, mine, 10, device(x, y, (z + d) & 7, c))

    ship(64, 128, IN_PARTS[2], send1, recv1, 2)

    @pl.when(z < 6)
    def _():
        wait(rsems.at[10], rows48.at[pl.ds(0, 40)])

    @pl.when(z >= 6)
    def _():
        wait(rsems.at[10], rows48)

    first = 192 * c + 48 * y
    diagonal = jnp.where(iota((48, N), 0) + first == iota((48, N), 1), jnp.broadcast_to(energies[...], (48, N)), 0.0)
    fock[pl.ds(pl.multiple_of(first, 48), 48), :] = (diagonal - rows48[...]).astype(BF16)
    mine = fock.at[pl.ds(pl.multiple_of(first, 48), 48)]
    for d in (1, 2, 3):
        start(mine, mine, 11, device(x, (y + d) & 3, z, c))
    ship(128, D, IN_PARTS[2], send1, recv1, 2)

    rho, nat = iota((N, N), 0), iota((N, N), 1)
    home = row_home(rho)
    gather = one_hot(home == nat)
    turn_t[...] = one_hot(home == lane_home(nat))
    turn[...] = one_hot(lane_home(rho) == row_home(nat))
    left = spread
    order = jnp.zeros((128, N), F32)
    for _ in range(3):
        piece = left.astype(BF16)
        left = left - piece.astype(F32)
        order = order + dot_t(piece, gather)
    upright = jnp.transpose(order)
    for t in range(3):
        lanes = slice(t * 128, t * 128 + 128)
        factor[:, lanes] = -(1.0 - upright - order[0:1, lanes])

    wait(rsems.at[11], fock.at[pl.ds(0, 144)])
    mine = fock.at[pl.ds(pl.multiple_of(192 * c, 192), 192)]
    start(mine, mine, 12, device(x, y, z, 1 - c))
    wait(rsems.at[12], mine)
    fock_p[...] = dot_t(dot(gather, fock[...]).astype(BF16), gather).astype(BF16)

    block = lax.broadcasted_iota(jnp.int16, (32, 128), 1)
    taken = recv1.reshape(UNITS, 2 * D, 128)
    given = send2.reshape(UNITS, 2 * D, 128)

    def spot(u, i):
        g = 16 * u + i
        return g // 36, g % 12 * 32, g // 12 % 3 * 128

    for j in range(K):
        wait(rsems.at[j], all_but_one(recv1, IN_PARTS[j]))
        for u in range(IN_PARTS[j][0], IN_PARTS[j][0] + IN_PARTS[j][1]):
            got = turn_blocks([taken[u, 32 * b : 32 * b + 32, :] for b in range(16)], block)
            for i in range(16):
                k, row, lane = spot(u, i)
                if k < K:
                    mats[k, row : row + 32, lane : lane + 128] = got[i]
        held = mats[j]
        anti = (dot(held, turn[...]) - dot_t(turn_t[...], held)).astype(BF16)
        both = dot(fock_p[...], anti) + dot_t(anti, fock_p[...])
        slope = (factor[...] * both).astype(BF16)
        outs[j] = dot(slope, turn_t[...]).astype(BF16)
        for u in range(OUT_PARTS[j][0], OUT_PARTS[j][0] + OUT_PARTS[j][1]):
            pieces = []
            for i in range(16):
                k, row, lane = spot(u, i)
                pieces.append(outs[k, row : row + 32, lane : lane + 128] if k < K else jnp.zeros((32, 128), BF16))
            got = turn_blocks(pieces, block)
            for b in range(16):
                given[u, 32 * b : 32 * b + 32, :] = got[b]
        ship(1, D, OUT_PARTS[j], send2, recv2, 3 + j)
    recv2[:, pl.ds(me, 1)] = send2[:, pl.ds(me, 1)]

    taken = recv2.reshape(UNITS, 2 * D, 128)
    for j in range(K):
        wait(rsems.at[3 + j], all_but_one(recv2, OUT_PARTS[j]))
        for u in range(OUT_PARTS[j][0], OUT_PARTS[j][0] + OUT_PARTS[j][1]):
            turned = dot(dot_t(eye, taken[u]).astype(BF16), mix[...])
            for i in range(2):
                zs[i, 128 * u : 128 * u + 128, :] = turned[:, i * D : (i + 1) * D]
    for h in range(0, BB, 2 * B):
        rows = []
        for t in range(0, 2 * B, 8):
            p, g = (h + t) // B, ((h + t) % B) // 8
            pieces = []
            for j in range(K):
                at = ((j * 3 + g) * 12 + p // 2) * 8
                pieces.append(zs[p % 2, at : at + 8, :])
            rows.append(jnp.concatenate(pieces, axis=1))
        out[h : h + 2 * B] = jnp.concatenate(rows, axis=0).astype(BF16).reshape(2 * B, 2, N)

    for j in range(K):
        wait(sems.at[j], all_but_one(send1, IN_PARTS[j]))
        wait(sems.at[3 + j], all_but_one(send2, OUT_PARTS[j]))
    wait(sems.at[6], from_core)
    wait(sems.at[7], from_y.at[pl.ds(0, 3)])

    @pl.when(z < 6)
    def _():
        wait(sems.at[8], from_z.at[pl.ds(0, 5)])
        wait(sems.at[9], from_x.at[pl.ds(0, 3)])
        wait(sems.at[10], from_z.at[pl.ds(0, 7)])

    @pl.when(z >= 6)
    def _():
        wait(sems.at[8], from_z.at[pl.ds(0, 6)])

    wait(sems.at[11], fock.at[pl.ds(0, 144)])
    wait(sems.at[12], fock.at[pl.ds(0, 192)])


def shards(amplitudes, prev_slope, cholesky_vectors, energies, occupations):
    vmem = pl.BlockSpec(memory_space=pltpu.VMEM)
    whole = pl.BlockSpec(memory_space=pl.ANY)
    slope = pl.pallas_call(
        kernel,
        out_shape=jax.ShapeDtypeStruct((BB, 2, N), BF16),
        in_specs=[whole] * 3 + [vmem] * 2,
        out_specs=vmem,
        scratch_shapes=[
            pltpu.VMEM((BB, 2, N), BF16),
            pltpu.VMEM((BB, 2, N), BF16),
            pltpu.VMEM((144 * B, N), BF16),
            pltpu.VMEM((2, UNITS * 128, D), F32),
            pltpu.VMEM((512, 512), BF16),
            pltpu.VMEM((512, 512), BF16),
            pltpu.VMEM((UNITS, D, 2, 128), BF16),
            pltpu.VMEM((UNITS, D, 2, 128), BF16),
            pltpu.VMEM((UNITS, D, 2, 128), BF16),
            pltpu.VMEM((UNITS, D, 2, 128), BF16),
            pltpu.VMEM((K, N, N), BF16),
            pltpu.VMEM((K, N, N), BF16),
            pltpu.VMEM((N, N), F32),
            pltpu.VMEM((N, N), F32),
            pltpu.VMEM((192, N), F32),
            pltpu.VMEM((48, N), F32),
            pltpu.VMEM((192, N), F32),
            pltpu.VMEM((4, 48, N), F32),
            pltpu.VMEM((8, 8, N), F32),
            pltpu.VMEM((4, 8, N), F32),
            pltpu.VMEM((48, N), F32),
            pltpu.VMEM((N, N), BF16),
            pltpu.VMEM((N, N), BF16),
            pltpu.VMEM((N, N), F32),
            pltpu.VMEM((N, N), BF16),
            pltpu.VMEM((N, N), BF16),
            pltpu.SemaphoreType.REGULAR,
            pltpu.SemaphoreType.DMA((3,)),
            pltpu.SemaphoreType.DMA((13,)),
            pltpu.SemaphoreType.DMA((13,)),
        ],
        compiler_params=pltpu.CompilerParams(
            collective_id=0, has_side_effects=True, vmem_limit_bytes=56 << 20
        ),
    )(
        amplitudes.reshape(BB, 2, N),
        prev_slope.reshape(BB, 2, N),
        cholesky_vectors.reshape(-1, N),
        energies,
        occupations,
    )
    return slope.reshape(B, B, 2, N)


def solution(mesh):
    in_specs = (P("pa", "pb", None, None), P("pa", "pb", None, None), P("pb", "pa", None), P(), P())
    out_specs = P("pa", "pb", None, None)
    return jax.shard_map(shards, mesh=mesh, in_specs=in_specs, out_specs=out_specs, check_vma=False)
```

time: 105 us -> 87.5 us (0.83)
  Pallas kernels: 97.4 us -> 84.7 us
  other arithmetic: 3.05 us -> 0 us
  local copies, waits for them, and re-layouts: 4.63 us -> 2.69 us
    pallas_call x1, Pallas kernels: 97.4 us -> 84.7 us  [shards(): pl.pallas_call(kernel, out_shape=jax.ShapeDtypeStruct((BB, 2, N), BF16),...]
    sub x3 -> x0, other arithmetic: 3.05 us -> none  [the longest x2 2.3 us: shards(): factor = 1.0 - occupations[:, None] - occupations[None, :]]
    reshape x1 -> x0, local copies, waits for them, and re-layouts: 1.26 us -> none  [shards(): energies.reshape(1, N)]
where the time goes in v3:
time: 87.5 us; the launch traced here: 87.4 us
  Pallas kernels  84.7 us (97%)
  local copies, waits for them, and re-layouts  2.69 us (3%)
    pallas_call x1, Pallas kernels, shards(): pl.pallas_call(kernel, out_shape=jax.ShapeDtypeStruct((BB, 2, N), BF16),...  84.7 us
    unnamed x1, local copies, waits for them, and re-layouts  2.69 us

profile of v3, /device:TPU:1, one launch (start us, length us, event | category | flops | bytes accessed | tf_op | source)
XLA Modules:
  0.0 87.4 jit_solution(17435425069541384368)
XLA Ops:
  0.0 84.7 %shard_map.55 = bf16[576,2,384]{2,1,0:T(2,128)(2,1)} custom-call(bf16[576,2,384]{2,1,0:T(2,128)(2,1)} %bitcast.6, bf16[576,2,384]{2,1,0:T(2,128)(2,1)} %bitcast.7, bf16[3456,384]{1,0:T(8,128)(2,1)} %bitcast.5, f32[384]{0:T(512)} %energies.1, f32[384]{0:T(512)} %occ.1), custom_call_target="tpu_custom_call" | custom-call | tf_op jit(solution)/shard_map/pallas_call | solution.py:317
  84.7 2.7 %copy.7 = bf16[24,24,2,384]{3,2,1,0:T(2,128)(2,1)} copy(bf16[24,24,2,384]{3,2,1,0:T(2,128)(2,1)} %bitcast.4) | data formatting | bytes 1769472

commit v4 on v3

--- a/solution.py
+++ b/solution.py
@@ -16,6 +16,8 @@
 MESH = pl.DeviceIdType.MESH
 IN_PARTS = ((0, 3), (3, 2), (5, 2))
 OUT_PARTS = ((0, 2), (2, 2), (4, 3))
+GAPS = (255, 128, 128, 254)
+TILES = 36
 
 
 def place():
@@ -71,7 +73,7 @@
 
 def kernel(amp_hbm, prev_hbm, chol_hbm, energies, occ, out,
            amp, prev, chol, zs, mix, mix_t, send1, recv1, send2, recv2, mats, outs, holes,
-           partial, half, sums, from_core, from_y, from_z, from_x, rows48, fock, fock_p, factor, turn, turn_t,
+           partial, half, from_core, from_xy, from_z, level, fock_tiles, fock, fock_p, factor, turn, turn_t,
            greet, loads, sems, rsems):
     x, y, z, c = place()
     me_a, me_b = device(x, y, z, c)
@@ -80,9 +82,9 @@
     load_amp = pltpu.make_async_copy(amp_hbm, amp, loads.at[0])
     load_prev = pltpu.make_async_copy(prev_hbm, prev, loads.at[1])
     load_chol = pltpu.make_async_copy(chol_hbm, chol, loads.at[2])
+    load_chol.start()
     load_amp.start()
     load_prev.start()
-    load_chol.start()
 
     barrier = pltpu.get_barrier_semaphore()
     column = [device(x, y, (z + d) & 7, c ^ e) for d in range(8) for e in range(2) if d or e]
@@ -108,6 +110,17 @@
 
         lax.fori_loop(lo, hi, step, 0)
 
+    queue = [(j, n) for j in range(K) for n in range(1, D)]
+    sent = [0]
+
+    def more(count):
+        todo = queue[sent[0] : sent[0] + count]
+        sent[0] += count
+        for j in range(K):
+            ns = [n for k, n in todo if k == j]
+            if ns:
+                ship(ns[0], ns[-1] + 1, IN_PARTS[j], send1, recv1, j)
+
     def all_but_one(buf, part):
         return buf.at[pl.ds(part[0], part[1]), pl.ds(0, D - 1)]
 
@@ -116,6 +129,32 @@
     mix_t[...] = one_hot((q >> 1) + (q & 1) * D == r)
     eye = one_hot(iota((128, 128), 0) == iota((128, 128), 1))
 
+    spread = jnp.broadcast_to(occ[...], (128, N))
+    upright = jnp.transpose(spread)
+    partial[:, 0:128] = upright
+    hole = 1.0 - 2.0 * partial[pl.ds(pl.multiple_of(me_a * B, 8), B), 0:128]
+    for i in range(16):
+        for t in range(3):
+            holes[i * B : (i + 1) * B, t * 128 : t * 128 + 128] = hole
+    load_chol.wait()
+    partial[...] = jnp.zeros((N, N), F32)
+
+    def rank_rows(i, _):
+        rows = chol[pl.ds(pl.multiple_of(i * 3 * N, N), 3 * N), :]
+        weighted = jnp.concatenate(
+            [(rows[t * N : (t + 1) * N].astype(F32) * holes[...]).astype(BF16) for t in range(3)], axis=0
+        )
+        partial[...] += lax.dot_general(
+            weighted, rows, (((0,), (0,)), ((), ())), preferred_element_type=F32
+        )
+        return 0
+
+    lax.fori_loop(0, 3, rank_rows, 0)
+
+    pl.semaphore_wait(barrier, len(column + plane))
+    for where in plane:
+        pl.semaphore_signal(greet, inc=1, device_id=where, device_id_type=MESH)
+    start(partial.at[pl.ds(192 * (1 - c), 192)], from_core, 6, device(x, y, z, 1 - c))
     load_amp.wait()
     load_prev.wait()
     for h in range(0, BB, 3 * B):
@@ -134,91 +173,24 @@
         folded[u] = dot_t(mix[...], pair).astype(BF16)
     recv1[:, pl.ds(me, 1)] = send1[:, pl.ds(me, 1)]
 
-    pl.semaphore_wait(barrier, len(column + plane))
-    for where in plane:
-        pl.semaphore_signal(greet, inc=1, device_id=where, device_id_type=MESH)
+    wait(rsems.at[6], from_core)
+    for t in range(TILES):
+        r, lanes = t // 3 * 16, slice(t % 3 * 128, t % 3 * 128 + 128)
+        half[t] = partial[pl.ds(192 * c + r, 16), lanes] + from_core[r : r + 16, lanes]
+    own = (x << 2) | y
+
+    def scatter(t, _):
+        o = t & 15
+
+        @pl.when(o != own)
+        def _():
+            start(half.at[t], from_xy.at[t >> 4, own], 7, device(o >> 2, o & 3, z, c))
+
+        return 0
+
+    lax.fori_loop(0, TILES, scatter, 0)
     pl.semaphore_wait(greet, len(plane))
-    ship(1, D, IN_PARTS[0], send1, recv1, 0)
-
-    spread = jnp.broadcast_to(occ[...], (128, N))
-    upright = jnp.transpose(spread)
-    partial[:, 0:128] = upright
-    hole = 1.0 - 2.0 * partial[pl.ds(pl.multiple_of(me_a * B, 8), B), 0:128]
-    for i in range(16):
-        for t in range(3):
-            holes[i * B : (i + 1) * B, t * 128 : t * 128 + 128] = hole
-    load_chol.wait()
-    partial[...] = jnp.zeros((N, N), F32)
-
-    def rank_rows(i, _):
-        rows = chol[pl.ds(pl.multiple_of(i * N, N), N), :]
-        weighted = (rows.astype(F32) * holes[...]).astype(BF16)
-        partial[...] += lax.dot_general(
-            weighted, rows, (((0,), (0,)), ((), ())), preferred_element_type=F32
-        )
-        return 0
-
-    lax.fori_loop(0, 9, rank_rows, 0)
-
-    start(partial.at[pl.ds(192 * (1 - c), 192)], from_core, 6, device(x, y, z, 1 - c))
-    ship(1, 64, IN_PARTS[1], send1, recv1, 1)
-    wait(rsems.at[6], from_core)
-    half[...] = partial[pl.ds(192 * c, 192), :] + from_core[...]
-    for d in (1, 2, 3):
-        y2 = (y + d) & 3
-        start(half.at[pl.ds(48 * y2, 48)], from_y.at[y], 7, device(x, y2, z, c))
-    from_y[pl.ds(y, 1)] = half[pl.ds(48 * y, 48), :][None]
-    ship(64, 192, IN_PARTS[1], send1, recv1, 1)
-    wait(rsems.at[7], from_y.at[pl.ds(0, 3)])
-    sums[...] = from_y[0] + from_y[1] + from_y[2] + from_y[3]
-    for d in range(1, 8):
-        z2 = (z + d) & 7
-
-        @pl.when(z2 < 6)
-        def _():
-            start(sums.at[pl.ds(8 * z2, 8)], from_z.at[z], 8, device(x, y, z2, c))
-
-    ship(192, D, IN_PARTS[1], send1, recv1, 1)
-
-    @pl.when(z < 6)
-    def _():
-        from_z[pl.ds(z, 1)] = sums[pl.ds(8 * z, 8), :][None]
-        wait(rsems.at[8], from_z.at[pl.ds(0, 7)])
-        total = from_z[0]
-        for d in range(1, 8):
-            total = total + from_z[d]
-        from_x[pl.ds(x, 1)] = total[None]
-        for d in (1, 2, 3):
-            start(from_x.at[x], from_x.at[x], 9, device((x + d) & 3, y, z, c))
-
-    ship(1, 64, IN_PARTS[2], send1, recv1, 2)
-
-    @pl.when(z < 6)
-    def _():
-        wait(rsems.at[9], from_x.at[pl.ds(0, 3)])
-        rows48[pl.ds(8 * z, 8), :] = from_x[0] + from_x[1] + from_x[2] + from_x[3]
-        for d in range(1, 8):
-            mine = rows48.at[pl.ds(8 * z, 8)]
-            start(mine, mine, 10, device(x, y, (z + d) & 7, c))
-
-    ship(64, 128, IN_PARTS[2], send1, recv1, 2)
-
-    @pl.when(z < 6)
-    def _():
-        wait(rsems.at[10], rows48.at[pl.ds(0, 40)])
-
-    @pl.when(z >= 6)
-    def _():
-        wait(rsems.at[10], rows48)
-
-    first = 192 * c + 48 * y
-    diagonal = jnp.where(iota((48, N), 0) + first == iota((48, N), 1), jnp.broadcast_to(energies[...], (48, N)), 0.0)
-    fock[pl.ds(pl.multiple_of(first, 48), 48), :] = (diagonal - rows48[...]).astype(BF16)
-    mine = fock.at[pl.ds(pl.multiple_of(first, 48), 48)]
-    for d in (1, 2, 3):
-        start(mine, mine, 11, device(x, (y + d) & 3, z, c))
-    ship(128, D, IN_PARTS[2], send1, recv1, 2)
-
+    more(GAPS[0])
     rho, nat = iota((N, N), 0), iota((N, N), 1)
     home = row_home(rho)
     gather = one_hot(home == nat)
@@ -235,11 +207,58 @@
         lanes = slice(t * 128, t * 128 + 128)
         factor[:, lanes] = -(1.0 - upright - order[0:1, lanes])
 
-    wait(rsems.at[11], fock.at[pl.ds(0, 144)])
-    mine = fock.at[pl.ds(pl.multiple_of(192 * c, 192), 192)]
-    start(mine, mine, 12, device(x, y, z, 1 - c))
-    wait(rsems.at[12], mine)
-    fock_p[...] = dot_t(dot(gather, fock[...]).astype(BF16), gather).astype(BF16)
+    more(GAPS[1])
+
+    @pl.when(own < 4)
+    def _():
+        wait(rsems.at[7], from_xy.at[pl.ds(0, 3), pl.ds(0, 15)])
+        from_xy[2, pl.ds(own, 1)] = half[pl.ds(32 + own, 1)]
+
+    @pl.when(own >= 4)
+    def _():
+        wait(rsems.at[7], from_xy.at[pl.ds(0, 2), pl.ds(0, 15)])
+        from_xy[2] = jnp.zeros((16, 16, 128), F32)
+
+    for k in range(2):
+        from_xy[k, pl.ds(own, 1)] = half[pl.ds(16 * k + own, 1)]
+    for k in range(3):
+        total = from_xy[k, 0]
+        for n in range(1, 16):
+            total = total + from_xy[k, n]
+        from_z[pl.ds(z, 1), k] = total[None]
+    for d in range(1, 8):
+        start(from_z.at[z], from_z.at[z], 8, device(x, y, (z + d) & 7, c))
+    more(GAPS[2])
+    for t in range(3):
+        level[t] = jnp.broadcast_to(energies[...], (16, N))[:, t * 128 : t * 128 + 128]
+    wait(rsems.at[8], from_z.at[pl.ds(0, 7)])
+
+    def finish(k):
+        total = from_z[0, k]
+        for n in range(1, 8):
+            total = total + from_z[n, k]
+        t = 16 * k + own
+        r, g = lax.div(t, 3), lax.rem(t, 3)
+        diagonal = iota((16, 128), 0) + 192 * c + 16 * r == iota((16, 128), 1) + 128 * g
+        shown = (jnp.where(diagonal, level[g], 0.0) - total).astype(BF16)
+        at = 36 * c + t
+        fock_tiles[pl.ds(at, 1)] = shown[None]
+
+        def tell(n, _):
+            to = device((x + (n >> 3)) & 3, (y + ((n >> 1) & 3)) & 3, z, (c + n) & 1)
+            start(fock_tiles.at[at], fock_tiles.at[at], 9, to)
+            return 0
+
+        lax.fori_loop(1, 32, tell, 0)
+
+    finish(0)
+    finish(1)
+
+    @pl.when(own < 4)
+    def _():
+        finish(2)
+
+    more(GAPS[3])
 
     block = lax.broadcasted_iota(jnp.int16, (32, 128), 1)
     taken = recv1.reshape(UNITS, 2 * D, 128)
@@ -258,7 +277,22 @@
                 if k < K:
                     mats[k, row : row + 32, lane : lane + 128] = got[i]
         held = mats[j]
-        anti = (dot(held, turn[...]) - dot_t(turn_t[...], held)).astype(BF16)
+        outs[j] = (dot(held, turn[...]) - dot_t(turn_t[...], held)).astype(BF16)
+
+    @pl.when(own < 4)
+    def _():
+        wait(rsems.at[9], fock_tiles.at[pl.ds(0, 69)])
+
+    @pl.when(own >= 4)
+    def _():
+        wait(rsems.at[9], fock_tiles.at[pl.ds(0, 70)])
+
+    for t in range(2 * TILES):
+        fock[t // 3 * 16 : t // 3 * 16 + 16, t % 3 * 128 : t % 3 * 128 + 128] = fock_tiles[t]
+    fock_p[...] = dot_t(dot(gather, fock[...]).astype(BF16), gather).astype(BF16)
+
+    for j in range(K):
+        anti = outs[j]
         both = dot(fock_p[...], anti) + dot_t(anti, fock_p[...])
         slope = (factor[...] * both).astype(BF16)
         outs[j] = dot(slope, turn_t[...]).astype(BF16)
@@ -295,20 +329,17 @@
         wait(sems.at[j], all_but_one(send1, IN_PARTS[j]))
         wait(sems.at[3 + j], all_but_one(send2, OUT_PARTS[j]))
     wait(sems.at[6], from_core)
-    wait(sems.at[7], from_y.at[pl.ds(0, 3)])
-
-    @pl.when(z < 6)
-    def _():
-        wait(sems.at[8], from_z.at[pl.ds(0, 5)])
-        wait(sems.at[9], from_x.at[pl.ds(0, 3)])
-        wait(sems.at[10], from_z.at[pl.ds(0, 7)])
-
-    @pl.when(z >= 6)
-    def _():
-        wait(sems.at[8], from_z.at[pl.ds(0, 6)])
-
-    wait(sems.at[11], fock.at[pl.ds(0, 144)])
-    wait(sems.at[12], fock.at[pl.ds(0, 192)])
+    wait(sems.at[8], from_z.at[pl.ds(0, 7)])
+
+    @pl.when(own < 4)
+    def _():
+        wait(sems.at[7], half.at[pl.ds(0, 33)])
+        wait(sems.at[9], send1.at[pl.ds(0, 3), pl.ds(0, 248)])
+
+    @pl.when(own >= 4)
+    def _():
+        wait(sems.at[7], half.at[pl.ds(0, 34)])
+        wait(sems.at[9], send1.at[pl.ds(0, 2), pl.ds(0, 248)])
 
 
 def shards(amplitudes, prev_slope, cholesky_vectors, energies, occupations):
@@ -334,13 +365,12 @@
             pltpu.VMEM((K, N, N), BF16),
             pltpu.VMEM((N, N), F32),
             pltpu.VMEM((N, N), F32),
+            pltpu.VMEM((TILES, 16, 128), F32),
             pltpu.VMEM((192, N), F32),
-            pltpu.VMEM((48, N), F32),
-            pltpu.VMEM((192, N), F32),
-            pltpu.VMEM((4, 48, N), F32),
-            pltpu.VMEM((8, 8, N), F32),
-            pltpu.VMEM((4, 8, N), F32),
-            pltpu.VMEM((48, N), F32),
+            pltpu.VMEM((3, 16, 16, 128), F32),
+            pltpu.VMEM((8, 3, 16, 128), F32),
+            pltpu.VMEM((3, 16, 128), F32),
+            pltpu.VMEM((2 * TILES, 16, 128), BF16),
             pltpu.VMEM((N, N), BF16),
             pltpu.VMEM((N, N), BF16),
             pltpu.VMEM((N, N), F32),
@@ -348,8 +378,8 @@
             pltpu.VMEM((N, N), BF16),
             pltpu.SemaphoreType.REGULAR,
             pltpu.SemaphoreType.DMA((3,)),
-            pltpu.SemaphoreType.DMA((13,)),
-            pltpu.SemaphoreType.DMA((13,)),
+            pltpu.SemaphoreType.DMA((10,)),
+            pltpu.SemaphoreType.DMA((10,)),
         ],
         compiler_params=pltpu.CompilerParams(
             collective_id=0, has_side_effects=True, vmem_limit_bytes=56 << 20

time: 87.5 us -> 79.6 us (0.910)
  Pallas kernels: 84.7 us -> 76.6 us
    pallas_call x1, Pallas kernels: 84.7 us -> 76.6 us  [shards(): pl.pallas_call(kernel, out_shape=jax.ShapeDtypeStruct((BB, 2, N), BF16),...]
where the time goes in v4:
time: 79.6 us; the launch traced here: 79.3 us
  Pallas kernels  76.6 us (96%)
  local copies, waits for them, and re-layouts  2.69 us (3%)
    pallas_call x1, Pallas kernels, shards(): pl.pallas_call(kernel, out_shape=jax.ShapeDtypeStruct((BB, 2, N), BF16),...  76.6 us
    unnamed x1, local copies, waits for them, and re-layouts  2.69 us

profile of v4, /device:TPU:1, one launch (start us, length us, event | category | flops | bytes accessed | tf_op | source)
XLA Modules:
  0.0 79.3 jit_solution(9721815482088632632)
XLA Ops:
  0.0 76.6 %shard_map.55 = bf16[576,2,384]{2,1,0:T(2,128)(2,1)} custom-call(bf16[576,2,384]{2,1,0:T(2,128)(2,1)} %bitcast.6, bf16[576,2,384]{2,1,0:T(2,128)(2,1)} %bitcast.7, bf16[3456,384]{1,0:T(8,128)(2,1)} %bitcast.5, f32[384]{0:T(512)} %energies.1, f32[384]{0:T(512)} %occ.1), custom_call_target="tpu_custom_call" | custom-call | tf_op jit(solution)/shard_map/pallas_call | solution.py:348
  76.6 2.7 %copy.7 = bf16[24,24,2,384]{3,2,1,0:T(2,128)(2,1)} copy(bf16[24,24,2,384]{3,2,1,0:T(2,128)(2,1)} %bitcast.4) | data formatting | bytes 1769472

commit v5 on v4

--- a/solution.py
+++ b/solution.py
@@ -16,8 +16,9 @@
 MESH = pl.DeviceIdType.MESH
 IN_PARTS = ((0, 3), (3, 2), (5, 2))
 OUT_PARTS = ((0, 2), (2, 2), (4, 3))
-GAPS = (255, 128, 128, 254)
-TILES = 36
+GAPS = (255, 255, 255, 0)
+TILES = 48
+UPPER = ((0, 0), (0, 1), (0, 2), (1, 1), (1, 2), (2, 2))
 
 
 def place():
@@ -73,7 +74,7 @@
 
 def kernel(amp_hbm, prev_hbm, chol_hbm, energies, occ, out,
            amp, prev, chol, zs, mix, mix_t, send1, recv1, send2, recv2, mats, outs, holes,
-           partial, half, from_core, from_xy, from_z, level, fock_tiles, fock, fock_p, factor, turn, turn_t,
+           partial, half, from_core, from_xy, from_z, fock_tiles, fock, fock_p, factor, turn, turn_t,
            greet, loads, sems, rsems):
     x, y, z, c = place()
     me_a, me_b = device(x, y, z, c)
@@ -154,7 +155,9 @@
     pl.semaphore_wait(barrier, len(column + plane))
     for where in plane:
         pl.semaphore_signal(greet, inc=1, device_id=where, device_id_type=MESH)
-    start(partial.at[pl.ds(192 * (1 - c), 192)], from_core, 6, device(x, y, z, 1 - c))
+    for n, (r, g) in enumerate(UPPER):
+        theirs = partial.at[pl.ds(pl.multiple_of(128 * r + 64 * (1 - c), 64), 64), pl.ds(128 * g, 128)]
+        start(theirs, from_core.at[n], 6, device(x, y, z, 1 - c))
     load_amp.wait()
     load_prev.wait()
     for h in range(0, BB, 3 * B):
@@ -174,9 +177,10 @@
     recv1[:, pl.ds(me, 1)] = send1[:, pl.ds(me, 1)]
 
     wait(rsems.at[6], from_core)
-    for t in range(TILES):
-        r, lanes = t // 3 * 16, slice(t % 3 * 128, t % 3 * 128 + 128)
-        half[t] = partial[pl.ds(192 * c + r, 16), lanes] + from_core[r : r + 16, lanes]
+    for n, (r, g) in enumerate(UPPER):
+        ours = partial[pl.ds(pl.multiple_of(128 * r + 64 * c, 64), 64), g * 128 : g * 128 + 128] + from_core[n]
+        for e in range(8):
+            half[8 * n + e] = ours[8 * e : 8 * e + 8]
     own = (x << 2) | y
 
     def scatter(t, _):
@@ -209,17 +213,8 @@
 
     more(GAPS[1])
 
-    @pl.when(own < 4)
-    def _():
-        wait(rsems.at[7], from_xy.at[pl.ds(0, 3), pl.ds(0, 15)])
-        from_xy[2, pl.ds(own, 1)] = half[pl.ds(32 + own, 1)]
-
-    @pl.when(own >= 4)
-    def _():
-        wait(rsems.at[7], from_xy.at[pl.ds(0, 2), pl.ds(0, 15)])
-        from_xy[2] = jnp.zeros((16, 16, 128), F32)
-
-    for k in range(2):
+    wait(rsems.at[7], from_xy.at[pl.ds(0, 3), pl.ds(0, 15)])
+    for k in range(3):
         from_xy[k, pl.ds(own, 1)] = half[pl.ds(16 * k + own, 1)]
     for k in range(3):
         total = from_xy[k, 0]
@@ -229,20 +224,14 @@
     for d in range(1, 8):
         start(from_z.at[z], from_z.at[z], 8, device(x, y, (z + d) & 7, c))
     more(GAPS[2])
-    for t in range(3):
-        level[t] = jnp.broadcast_to(energies[...], (16, N))[:, t * 128 : t * 128 + 128]
     wait(rsems.at[8], from_z.at[pl.ds(0, 7)])
 
     def finish(k):
         total = from_z[0, k]
         for n in range(1, 8):
             total = total + from_z[n, k]
-        t = 16 * k + own
-        r, g = lax.div(t, 3), lax.rem(t, 3)
-        diagonal = iota((16, 128), 0) + 192 * c + 16 * r == iota((16, 128), 1) + 128 * g
-        shown = (jnp.where(diagonal, level[g], 0.0) - total).astype(BF16)
-        at = 36 * c + t
-        fock_tiles[pl.ds(at, 1)] = shown[None]
+        at = TILES * c + 16 * k + own
+        fock_tiles[pl.ds(at, 1)] = total[None]
 
         def tell(n, _):
             to = device((x + (n >> 3)) & 3, (y + ((n >> 1) & 3)) & 3, z, (c + n) & 1)
@@ -251,12 +240,8 @@
 
         lax.fori_loop(1, 32, tell, 0)
 
-    finish(0)
-    finish(1)
-
-    @pl.when(own < 4)
-    def _():
-        finish(2)
+    for k in range(3):
+        finish(k)
 
     more(GAPS[3])
 
@@ -279,16 +264,17 @@
         held = mats[j]
         outs[j] = (dot(held, turn[...]) - dot_t(turn_t[...], held)).astype(BF16)
 
-    @pl.when(own < 4)
-    def _():
-        wait(rsems.at[9], fock_tiles.at[pl.ds(0, 69)])
-
-    @pl.when(own >= 4)
-    def _():
-        wait(rsems.at[9], fock_tiles.at[pl.ds(0, 70)])
-
-    for t in range(2 * TILES):
-        fock[t // 3 * 16 : t // 3 * 16 + 16, t % 3 * 128 : t % 3 * 128 + 128] = fock_tiles[t]
+    wait(rsems.at[9], fock_tiles.at[pl.ds(0, 2 * TILES - 3)])
+    level = jnp.broadcast_to(energies[...], (128, N))
+    diagonal = iota((128, 128), 0) == iota((128, 128), 1)
+    for n, (r, g) in enumerate(UPPER):
+        total = jnp.concatenate([fock_tiles[TILES * e + 8 * n + d] for e in range(2) for d in range(8)], axis=0)
+        rows, lanes = slice(r * 128, r * 128 + 128), slice(g * 128, g * 128 + 128)
+        if r == g:
+            fock[rows, lanes] = (jnp.where(diagonal, level[:, lanes], 0.0) - total).astype(BF16)
+        else:
+            fock[rows, lanes] = (0.0 - total).astype(BF16)
+            fock[lanes, rows] = (0.0 - jnp.transpose(total)).astype(BF16)
     fock_p[...] = dot_t(dot(gather, fock[...]).astype(BF16), gather).astype(BF16)
 
     for j in range(K):
@@ -329,17 +315,9 @@
         wait(sems.at[j], all_but_one(send1, IN_PARTS[j]))
         wait(sems.at[3 + j], all_but_one(send2, OUT_PARTS[j]))
     wait(sems.at[6], from_core)
+    wait(sems.at[7], half.at[pl.ds(0, 45)])
     wait(sems.at[8], from_z.at[pl.ds(0, 7)])
-
-    @pl.when(own < 4)
-    def _():
-        wait(sems.at[7], half.at[pl.ds(0, 33)])
-        wait(sems.at[9], send1.at[pl.ds(0, 3), pl.ds(0, 248)])
-
-    @pl.when(own >= 4)
-    def _():
-        wait(sems.at[7], half.at[pl.ds(0, 34)])
-        wait(sems.at[9], send1.at[pl.ds(0, 2), pl.ds(0, 248)])
+    wait(sems.at[9], fock_tiles.at[pl.ds(0, 2 * TILES - 3)])
 
 
 def shards(amplitudes, prev_slope, cholesky_vectors, energies, occupations):
@@ -365,12 +343,11 @@
             pltpu.VMEM((K, N, N), BF16),
             pltpu.VMEM((N, N), F32),
             pltpu.VMEM((N, N), F32),
-            pltpu.VMEM((TILES, 16, 128), F32),
-            pltpu.VMEM((192, N), F32),
-            pltpu.VMEM((3, 16, 16, 128), F32),
-            pltpu.VMEM((8, 3, 16, 128), F32),
-            pltpu.VMEM((3, 16, 128), F32),
-            pltpu.VMEM((2 * TILES, 16, 128), BF16),
+            pltpu.VMEM((TILES, 8, 128), F32),
+            pltpu.VMEM((6, 64, 128), F32),
+            pltpu.VMEM((3, 16, 8, 128), F32),
+            pltpu.VMEM((8, 3, 8, 128), F32),
+            pltpu.VMEM((2 * TILES, 8, 128), F32),
             pltpu.VMEM((N, N), BF16),
             pltpu.VMEM((N, N), BF16),
             pltpu.VMEM((N, N), F32),

time: 79.6 us -> 74.9 us (0.941)
  Pallas kernels: 76.6 us -> 72.1 us
    pallas_call x1, Pallas kernels: 76.6 us -> 72.1 us  [shards(): pl.pallas_call(kernel, out_shape=jax.ShapeDtypeStruct((BB, 2, N), BF16),...]
where the time goes in v5:
time: 74.9 us; the launch traced here: 74.8 us
  Pallas kernels  72.1 us (96%)
  local copies, waits for them, and re-layouts  2.69 us (4%)
    pallas_call x1, Pallas kernels, shards(): pl.pallas_call(kernel, out_shape=jax.ShapeDtypeStruct((BB, 2, N), BF16),...  72.1 us
    unnamed x1, local copies, waits for them, and re-layouts  2.69 us

profile of v5, /device:TPU:1, one launch (start us, length us, event | category | flops | bytes accessed | tf_op | source)
XLA Modules:
  0.0 74.8 jit_solution(1342766747788090988)
XLA Ops:
  0.0 72.1 %shard_map.55 = bf16[576,2,384]{2,1,0:T(2,128)(2,1)} custom-call(bf16[576,2,384]{2,1,0:T(2,128)(2,1)} %bitcast.6, bf16[576,2,384]{2,1,0:T(2,128)(2,1)} %bitcast.7, bf16[3456,384]{1,0:T(8,128)(2,1)} %bitcast.5, f32[384]{0:T(512)} %energies.1, f32[384]{0:T(512)} %occ.1), custom_call_target="tpu_custom_call" | custom-call | tf_op jit(solution)/shard_map/pallas_call | solution.py:326
  72.1 2.7 %copy.7 = bf16[24,24,2,384]{3,2,1,0:T(2,128)(2,1)} copy(bf16[24,24,2,384]{3,2,1,0:T(2,128)(2,1)} %bitcast.4) | data formatting | bytes 1769472
